TPU v7x, 32 devices: a whole 2x2x4 slice. The times are simulated.
32 devices in a mesh: tm: 2 (over x), tile: 16 (over z, y, core).
Axes of the slice: x: 2, y: 2, z: 4, core: 2. Of those that a mesh axis runs over, the one named last changes fastest.
Arguments:
- starts: float32 [2, 24576, 128], P('tm', 'tile'), may hold values from -6 to 6
- sources: float32 [24576, 128], P('tile'), may hold values from -6 to 6
- fine_ops: float32 [2, 192, 4, 128, 128], P('tm', 'tile'), may hold values from -0.1875 to 0.1875
- col_index: int32 [2, 192, 4], P('tm', 'tile'), may hold values from 0 to 15, as said below
- live_count: int32 [2, 192], P('tm', 'tile'), may hold values from 1 to 4, as said below
- coarse_op: float32 [6144, 768], P('tile'), may hold values from -0.15625 to 0.15625
- cell_map: int32 [24576], P('tile'), may hold values from 0 to 383, as said below
Outputs:
- corrected: float32 [2, 24576, 128], P('tm', 'tile')
Inputs may be any that keep to these rules, and one draw needn't show every extreme that they name: `col_index`: each entry names one of the 16 blocks of a tile's fine window. Slots from live_count on are padding and carry no transport. `cell_map`: each entry is a local coarse index within its own tile; every coarse cell of every tile has at least one fine cell.
All inputs are finite; a program needn't handle non-finite values.
Results may differ from a plain program's by a relative error of at most 0.0003.
Values sent between devices are 32-bit elements; how exact they have to be, the bound alone decides.
A program may use at most 64 MiB of HBM per device.

v0:
```python
import jax
import jax.numpy as jnp
from jax import lax
from jax.sharding import PartitionSpec as P

HALO = 256
STEPS = 2


def extended_2(cells, sides, width):
    for axis, dim in sides:
        count = lax.axis_size(axis)
        head = lax.slice_in_dim(cells, 0, width, axis=dim)
        tail = lax.slice_in_dim(cells, cells.shape[dim] - width, cells.shape[dim], axis=dim)
        cells = jnp.concatenate(
            [
                lax.ppermute(tail, axis, [(i, (i + 1) % count) for i in range(count)]),
                cells,
                lax.ppermute(head, axis, [((i + 1) % count, i) for i in range(count)]),
            ],
            axis=dim,
        )
    return cells


def passed_along(block, axis, distance):
    devices = range(lax.axis_size(axis))
    route = [(i - distance, i) for i in devices if i - distance in devices]
    return lax.ppermute(block, axis, route)


def on_device(starts, sources, fine_ops, col_index, live_count, coarse_op, cell_map):
    first_state = starts[0]
    transport = fine_ops[0]
    columns = col_index[0]
    slot_counts = live_count[0]
    row_count, tracers = first_state.shape
    slot_total = transport.shape[1]
    block_size = transport.shape[2]
    coarse = coarse_op.shape[0]
    coarse_rim = (coarse_op.shape[1] - coarse) // 2
    live_mask = (jnp.arange(slot_total)[None, :] < slot_counts[:, None]).astype(jnp.float32)
    fine_end = first_state
    for step_index in range(STEPS):
        fine_extended = extended_2(fine_end, (("tile", 0),), HALO)
        pieces = (
            fine_extended.reshape(-1, block_size, tracers)[columns] * live_mask[:, :, None, None]
        )
        transported = jnp.einsum(
            "bkij,bkjn->bin", transport, pieces, precision=lax.Precision.HIGHEST
        )
        fine_end = transported.reshape(row_count, tracers) + sources
    onehot = (cell_map[:, None] == jnp.arange(coarse, dtype=jnp.int32)[None, :]).astype(jnp.float32)
    children = jnp.sum(onehot, axis=0)

    def restrict(values_in):
        sums = lax.dot_general(
            onehot, values_in, (((0,), (0,)), ((), ())), precision=lax.Precision.HIGHEST
        )
        return sums / children[:, None]

    following = passed_along(restrict(first_state), "tm", -1)
    jump_term = restrict(fine_end) - following

    def coarse_apply(coarse_state):
        extended = extended_2(coarse_state, (("tile", 0),), coarse_rim)
        return jnp.dot(coarse_op, extended, precision=lax.Precision.HIGHEST)

    slice_count = lax.axis_size("tm")
    empty_coarse = jnp.zeros((coarse, tracers), jnp.float32)

    def advance(step_index, current):
        return passed_along(coarse_apply(current) + jump_term, "tm", 1)

    current = lax.fori_loop(0, slice_count - 1, advance, empty_coarse)
    carried = coarse_apply(current)
    result = fine_end + jnp.dot(onehot, carried, precision=lax.Precision.HIGHEST)
    return result[None]


def solution(mesh):
    placed = (
        P("tm", "tile", None),
        P("tile", None),
        P("tm", "tile", None, None, None),
        P("tm", "tile", None),
        P("tm", "tile"),
        P("tile", None),
        P("tile"),
    )
    return jax.shard_map(
        on_device, mesh=mesh, in_specs=placed, out_specs=P("tm", "tile", None), check_vma=False
    )
```

profile of v0, /device:TPU:31, one launch (start us, length us, event | category | flops | bytes accessed | tf_op | source)
XLA Modules:
  0.0 67.3 jit_solution(16588640380827401001)
XLA Ops:
  0.0 0.0 copy-start
  0.0 0.7 slice.36
  0.7 0.4 collective-permute-start.4
  1.1 0.2 collective-permute-start.5
  1.3 1.6 %slice_bitcast_fusion.1 = (f32[256,128]{1,0:T(8,128)}, f32[256,128]{1,0:T(8,128)S(1)}) fusion(f32[1,1536,128]{2,1,0:T(8,128)} %param.7), kind=kLoop, calls=%fused_computation.40 | loop fusion | bytes 524288 | tf_op jit(solution)/shard_map/slice | solution.py:14
  3.0 4.2 %collective-permute-start = (f32[256,128]{1,0:T(8,128)}, f32[256,128]{1,0:T(8,128)S(1)}, u32[]{:S(2)}, u32[]{:S(2)}) collective-permute-start(f32[256,128]{1,0:T(8,128)} %get-tuple-element.18), channel_id=1, source_target_pairs={{0,1},{1,2},{2,3},{3,4},{4,5},{5,6},{6,7},{7,8},{8,9},{9,10},{10,1... | collective-permute-start | bytes 393224 | tf_op jit(solution)/shard_map/ppermute | solution.py:17
  7.2 0.0 collective-permute-start.1
  7.2 0.7 %compare_select_fusion = s32[12,4,1]{0,1,2:T(4,128)S(1)} fusion(s32[1,12,4]{1,2,0:T(4,128)} %param.10), kind=kLoop, calls=%fused_computation.43 | loop fusion | flops 144 | bytes 384 | tf_op jit(solution)/shard_map/select_n | solution.py:47
  7.9 0.1 copy.14
  8.0 0.1 reshape.75
  8.1 0.7 %fusion.29 = f32[12,4]{1,0:T(8,128)S(1)} fusion(s32[12]{0:T(128)} %bitcast.50), kind=kLoop, calls=%fused_computation.42 | loop fusion | flops 96 | bytes 240 | tf_op jit(solution)/shard_map/convert_element_type | solution.py:42
  8.8 1.0 %convert_reduce_fusion = f32[384]{0:T(512)S(1)} fusion(s32[1536]{0:T(1024)} %param.13), kind=kLoop, calls=%fused_computation.10 | loop fusion | flops 1769088 | bytes 7680 | tf_op jit(solution)/shard_map/reduce_sum | solution.py:54
  9.8 0.0 collective-permute-done
  9.8 4.5 %collective-permute-done.1 = f32[256,128]{1,0:T(8,128)S(1)} collective-permute-done((f32[256,128]{1,0:T(8,128)S(1)}, f32[256,128]{1,0:T(8,128)S(1)}, u32[]{:S(2)}, u32[]{:S(2)}) %collective-permute-start.1) | collective-permute-done | bytes 131104 | tf_op jit(solution)/shard_map/ppermute | solution.py:19
  14.3 2.2 %pad_maximum_fusion = f32[2048,128]{1,0:T(8,128)} fusion(f32[256,128]{1,0:T(8,128)S(1)} %collective-permute-done.1, f32[1536,128]{1,0:T(8,128)} %bitcast.49, f32[256,128]{1,0:T(8,128)S(1)} %collective-permute-done), kind=kLoop, calls=%fused_computation.24 | loop fusion | flops 524288 | bytes 2097152 | tf_op jit(solution)/shard_map/concatenate | solution.py:15
  16.5 3.6 %gather_fusion = f32[48,128,128]{2,1,0:T(8,128)} fusion(f32[16,128,128]{2,1,0:T(8,128)} %bitcast.46, s32[1024]{0:T(1024)S(1)} %pad_clamp_fusion), kind=kCustom, calls=%fused_computation | custom fusion | bytes 6291648 | tf_op jit(solution)/shard_map/gather | solution.py:47
  20.1 0.0 copy-done
  20.1 5.7 %fusion.2 = f32[12,128,128,1]{1,2,3,0:T(8,128)S(1)} fusion(f32[1,12,4,128,128]{4,3,2,1,0:T(8,128)S(1)} %copy-done, f32[12,4,128,128]{3,2,1,0:T(8,128)} %bitcast.48, f32[12,4]{1,0:T(8,128)S(1)} %fusion.29), kind=kOutput, calls=%fused_computation.4 | convolution fusion | flops 1208745984 | bytes 7078080 | tf_op jit(solution)/shard_map/bkij,bkjn->bin/dot_general | solution.py:49
  25.8 0.0 copy-done.2
  25.8 0.1 bitcast_add_fusion.1
  26.0 0.3 collective-permute-start.2
  26.2 0.3 collective-permute-start.3
  26.5 0.0 copy-done.4
  26.5 1.9 %fusion.15 = f32[384,128]{0,1:T(8,128)} fusion(s32[1536]{0:T(1024)S(1)} %copy-done.5, f32[384]{0:T(512)S(1)} %convert_reduce_fusion, f32[1,1536,128]{2,1,0:T(8,128)S(1)} %copy-done.4), kind=kOutput, calls=%fused_computation.20 | convolution fusion | flops 906608640 | bytes 990720 | tf_op jit(solution)/shard_map/dot_general | solution.py:57
  28.5 1.9 %collective-permute-start.6 = (f32[384,128]{0,1:T(8,128)}, f32[384,128]{0,1:T(8,128)S(1)}, u32[]{:S(2)}, u32[]{:S(2)}) collective-permute-start(f32[384,128]{0,1:T(8,128)} %fusion.15), channel_id=1, source_target_pairs={{16,0},{17,1},{18,2},{19,3},{20,4},{21,5},{22,6},{23,7},{24,8},{25... | collective-permute-start | bytes 589832 | tf_op jit(solution)/shard_map/ppermute | solution.py:29
  30.4 0.1 pad.4.clone
  30.5 0.0 collective-permute-done.2
  30.5 2.8 %collective-permute-done.3 = f32[256,128]{1,0:T(8,128)S(1)} collective-permute-done((f32[256,128]{1,0:T(8,128)S(1)}, f32[256,128]{1,0:T(8,128)S(1)}, u32[]{:S(2)}, u32[]{:S(2)}) %collective-permute-start.3) | collective-permute-done | bytes 131104 | tf_op jit(solution)/shard_map/ppermute | solution.py:19
  33.3 1.1 %pad_maximum_fusion.1 = f32[2048,128]{1,0:T(8,128)} fusion(f32[256,128]{1,0:T(8,128)S(1)} %collective-permute-done.3, f32[1536,128]{1,0:T(8,128)S(1)} %bitcast_add_fusion.1, f32[256,128]{1,0:T(8,128)S(1)} %collective-permute-done.2), kind=kLoop, calls=%fused_computation.25 | loop fusion | flops 524288 | bytes 2097152 | tf_op jit(solution)/shard_map/concatenate | solution.py:15
  34.4 3.6 %gather_fusion.1 = f32[48,128,128]{2,1,0:T(8,128)} fusion(f32[16,128,128]{2,1,0:T(8,128)} %bitcast.45, s32[1024]{0:T(1024)S(1)} %pad_clamp_fusion), kind=kCustom, calls=%fused_computation.1 | custom fusion | bytes 6291648 | tf_op jit(solution)/shard_map/gather | solution.py:47
  38.0 5.6 %fusion = f32[12,128,128,1]{1,2,3,0:T(8,128)S(1)} fusion(f32[1,12,4,128,128]{4,3,2,1,0:T(8,128)S(1)} %copy-done, f32[12,4,128,128]{3,2,1,0:T(8,128)} %bitcast.47, f32[12,4]{1,0:T(8,128)S(1)} %fusion.29), kind=kOutput, calls=%fused_computation.2 | convolution fusion | flops 1208745984 | bytes 7078080 | tf_op jit(solution)/shard_map/bkij,bkjn->bin/dot_general | solution.py:49
  43.7 0.0 copy-start.1
  43.7 0.1 bitcast_add_fusion
  43.8 0.0 collective-permute-done.6
  43.8 1.3 %fusion.16 = f32[384,128]{0,1:T(8,128)S(1)} fusion(f32[384,128]{0,1:T(8,128)S(1)} %collective-permute-done.6, f32[1536,128]{1,0:T(8,128)S(1)} %bitcast_add_fusion, s32[1536]{0:T(1024)S(1)} %copy-done.5, f32[384]{0:T(512)S(1)} %convert_reduce_fusion), kind=kOutput, calls=%fused_computation.21 | convolution fusion | flops 906657792 | bytes 1187328 | tf_op jit(solution)/shard_map/dot_general | solution.py:57
  45.1 0.0 collective-permute-done.4
  45.1 0.0 collective-permute-done.5
  45.1 0.0 copy-done.1
  45.1 2.5 %fusion.17 = f32[384,128]{0,1:T(8,128)S(1)} fusion(f32[384,128]{0,1:T(8,128)S(1)} %fusion.16, f32[384,768]{1,0:T(8,128)S(1)} %copy-done.1, f32[192,128]{1,0:T(8,128)} %collective-permute-done.5, f32[192,128]{1,0:T(8,128)} %collective-permute-done.4, f32[768]{0:T(1024)S(1)} %pad.4.clone), kind=kOutput, calls=%fused_computation.23 | convolution fusion | flops 453230592 | bytes 1772544 | tf_op jit(solution)/shard_map/while/body/eval_jaxpr/dot_general | solution.py:67
  47.6 1.3 %collective-permute-start.7 = (f32[384,128]{0,1:T(8,128)S(1)}, f32[384,128]{0,1:T(8,128)S(1)}, u32[]{:S(2)}, u32[]{:S(2)}) collective-permute-start(f32[384,128]{0,1:T(8,128)S(1)} %fusion.17), channel_id=1, source_target_pairs={{0,16},{1,17},{2,18},{3,19},{4,20},{5,21},{6,22},{7,23},{8,24},{9,... | collective-permute-start | bytes 589832 | tf_op jit(solution)/shard_map/while/body/eval_jaxpr/ppermute | solution.py:29
  48.9 5.1 %collective-permute-done.7 = f32[384,128]{0,1:T(8,128)S(1)} collective-permute-done((f32[384,128]{0,1:T(8,128)S(1)}, f32[384,128]{0,1:T(8,128)S(1)}, u32[]{:S(2)}, u32[]{:S(2)}) %collective-permute-start.7) | collective-permute-done | bytes 196640 | tf_op jit(solution)/shard_map/while/body/eval_jaxpr/ppermute | solution.py:29
  54.0 0.1 fusion.34
  54.1 2.8 %collective-permute-start.8 = (f32[192,128]{0,1:T(8,128)S(1)}, f32[192,128]{0,1:T(8,128)S(1)}, u32[]{:S(2)}, u32[]{:S(2)}) collective-permute-start(f32[192,128]{0,1:T(8,128)S(1)} %get-tuple-element.21), channel_id=1, source_target_pairs={{0,1},{1,2},{2,3},{3,4},{4,5},{5,6},{6,7},{7,8},{8,9},{9,10},{10,1... | collective-permute-start | bytes 294920 | tf_op jit(solution)/shard_map/ppermute | solution.py:17
  56.9 0.0 collective-permute-start.9
  56.9 1.9 %collective-permute-done.8 = f32[192,128]{0,1:T(8,128)S(1)} collective-permute-done((f32[192,128]{0,1:T(8,128)S(1)}, f32[192,128]{0,1:T(8,128)S(1)}, u32[]{:S(2)}, u32[]{:S(2)}) %collective-permute-start.8) | collective-permute-done | bytes 98336 | tf_op jit(solution)/shard_map/ppermute | solution.py:17
  58.9 5.1 %collective-permute-done.9 = f32[192,128]{0,1:T(8,128)S(1)} collective-permute-done((f32[192,128]{0,1:T(8,128)S(1)}, f32[192,128]{0,1:T(8,128)S(1)}, u32[]{:S(2)}, u32[]{:S(2)}) %collective-permute-start.9) | collective-permute-done | bytes 98336 | tf_op jit(solution)/shard_map/ppermute | solution.py:19
  64.0 1.2 %fusion.22 = f32[128,384]{1,0:T(8,128)S(1)} fusion(f32[384,768]{1,0:T(8,128)S(1)} %copy-done.1, f32[192,128]{0,1:T(8,128)S(1)} %collective-permute-done.9, f32[384,128]{0,1:T(8,128)S(1)} %collective-permute-done.7, f32[192,128]{0,1:T(8,128)S(1)} %collective-permute-done.8), kind=kOutput, calls=%fused_computation.32 | convolution fusion | flops 453181440 | bytes 1769472 | tf_op jit(solution)/shard_map/dot_general | solution.py:67
  65.2 2.1 %fusion.6 = f32[1,1536,128]{2,1,0:T(8,128)} fusion(f32[1536,128]{1,0:T(8,128)S(1)} %bitcast_add_fusion, f32[128,384]{1,0:T(8,128)S(1)} %fusion.22, s32[1536]{0:T(1024)S(1)} %copy-done.5), kind=kOutput, calls=%fused_computation.9 | convolution fusion | flops 906756096 | bytes 1775616 | tf_op jit(solution)/shard_map/dot_general | solution.py:77
  (9 shorter events, 0.0 us)
Async XLA Ops:
  0.0 20.1 %copy-start = (f32[1,12,4,128,128]{4,3,2,1,0:T(8,128)S(1)}, f32[1,12,4,128,128]{4,3,2,1,0:T(8,128)}, u32[]{:S(2)}) copy-start(f32[1,12,4,128,128]{4,3,2,1,0:T(8,128)} %param.9) | copy-start | bytes 9437188
  0.7 44.4 %collective-permute-start.4 = (f32[192,128]{1,0:T(8,128)}, f32[192,128]{1,0:T(8,128)}, u32[]{:S(2)}, u32[]{:S(2)}) collective-permute-start(f32[192,128]{1,0:T(8,128)} %slice.36), channel_id=1, source_target_pairs={{0,1},{1,2},{2,3},{3,4},{4,5},{5,6},{6,7},{7,8},{8,9},{9,10},{10,1... | collective-permute-start | bytes 294920 | tf_op jit(solution)/shard_map/while/body/eval_jaxpr/ppermute | solution.py:17
  1.1 44.0 %collective-permute-start.5 = (f32[192,128]{1,0:T(8,128)}, f32[192,128]{1,0:T(8,128)}, u32[]{:S(2)}, u32[]{:S(2)}) collective-permute-start(f32[192,128]{1,0:T(8,128)} %slice.36), channel_id=1, source_target_pairs={{1,0},{2,1},{3,2},{4,3},{5,4},{6,5},{7,6},{8,7},{9,8},{10,9},{11,1... | collective-permute-start | bytes 294920 | tf_op jit(solution)/shard_map/while/body/eval_jaxpr/ppermute | solution.py:19
  3.0 6.8 %collective-permute-start = (f32[256,128]{1,0:T(8,128)}, f32[256,128]{1,0:T(8,128)S(1)}, u32[]{:S(2)}, u32[]{:S(2)}) collective-permute-start(f32[256,128]{1,0:T(8,128)} %get-tuple-element.18), channel_id=1, source_target_pairs={{0,1},{1,2},{2,3},{3,4},{4,5},{5,6},{6,7},{7,8},{8,9},{9,10},{10,1... | collective-permute-start | bytes 393224 | tf_op jit(solution)/shard_map/ppermute | solution.py:17
  7.2 7.1 %collective-permute-start.1 = (f32[256,128]{1,0:T(8,128)S(1)}, f32[256,128]{1,0:T(8,128)S(1)}, u32[]{:S(2)}, u32[]{:S(2)}) collective-permute-start(f32[256,128]{1,0:T(8,128)S(1)} %get-tuple-element.20), channel_id=1, source_target_pairs={{1,0},{2,1},{3,2},{4,3},{5,4},{6,5},{7,6},{8,7},{9,8},{10,9},{11,1... | collective-permute-start | bytes 393224 | tf_op jit(solution)/shard_map/ppermute | solution.py:19
  20.1 5.7 %copy-start.2 = (f32[1536,128]{1,0:T(8,128)S(1)}, f32[1536,128]{1,0:T(8,128)}, u32[]{:S(2)}) copy-start(f32[1536,128]{1,0:T(8,128)} %param.8) | copy-start | bytes 2359300
  20.1 6.4 %copy-start.4 = (f32[1,1536,128]{2,1,0:T(8,128)S(1)}, f32[1,1536,128]{2,1,0:T(8,128)}, u32[]{:S(2)}) copy-start(f32[1,1536,128]{2,1,0:T(8,128)} %param.7) | copy-start | bytes 2359300
  20.1 6.4 %copy-start.5 = (s32[1536]{0:T(1024)S(1)}, s32[1536]{0:T(1024)}, u32[]{:S(2)}) copy-start(s32[1536]{0:T(1024)} %param.13) | copy-start | bytes 18436
  26.0 4.5 %collective-permute-start.2 = (f32[256,128]{1,0:T(8,128)S(1)}, f32[256,128]{1,0:T(8,128)S(1)}, u32[]{:S(2)}, u32[]{:S(2)}) collective-permute-start(f32[256,128]{1,0:T(8,128)S(1)} %get-tuple-element.11), channel_id=1, source_target_pairs={{0,1},{1,2},{2,3},{3,4},{4,5},{5,6},{6,7},{7,8},{8,9},{9,10},{10,1... | collective-permute-start | bytes 393224 | tf_op jit(solution)/shard_map/ppermute | solution.py:17
  26.2 7.1 %collective-permute-start.3 = (f32[256,128]{1,0:T(8,128)S(1)}, f32[256,128]{1,0:T(8,128)S(1)}, u32[]{:S(2)}, u32[]{:S(2)}) collective-permute-start(f32[256,128]{1,0:T(8,128)S(1)} %get-tuple-element.16), channel_id=1, source_target_pairs={{1,0},{2,1},{3,2},{4,3},{5,4},{6,5},{7,6},{8,7},{9,8},{10,9},{11,1... | collective-permute-start | bytes 393224 | tf_op jit(solution)/shard_map/ppermute | solution.py:19
  28.5 15.3 %collective-permute-start.6 = (f32[384,128]{0,1:T(8,128)}, f32[384,128]{0,1:T(8,128)S(1)}, u32[]{:S(2)}, u32[]{:S(2)}) collective-permute-start(f32[384,128]{0,1:T(8,128)} %fusion.15), channel_id=1, source_target_pairs={{16,0},{17,1},{18,2},{19,3},{20,4},{21,5},{22,6},{23,7},{24,8},{25... | collective-permute-start | bytes 589832 | tf_op jit(solution)/shard_map/ppermute | solution.py:29
  38.0 5.7 %copy-start.3 = (f32[1536,128]{1,0:T(8,128)S(1)}, f32[1536,128]{1,0:T(8,128)}, u32[]{:S(2)}) copy-start(f32[1536,128]{1,0:T(8,128)} %param.8) | copy-start | bytes 2359300
  43.7 1.4 %copy-start.1 = (f32[384,768]{1,0:T(8,128)S(1)}, f32[384,768]{1,0:T(8,128)}, u32[]{:S(2)}) copy-start(f32[384,768]{1,0:T(8,128)} %param.12) | copy-start | bytes 3538948
  47.6 6.4 %collective-permute-start.7 = (f32[384,128]{0,1:T(8,128)S(1)}, f32[384,128]{0,1:T(8,128)S(1)}, u32[]{:S(2)}, u32[]{:S(2)}) collective-permute-start(f32[384,128]{0,1:T(8,128)S(1)} %fusion.17), channel_id=1, source_target_pairs={{0,16},{1,17},{2,18},{3,19},{4,20},{5,21},{6,22},{7,23},{8,24},{9,... | collective-permute-start | bytes 589832 | tf_op jit(solution)/shard_map/while/body/eval_jaxpr/ppermute | solution.py:29
  54.1 4.7 %collective-permute-start.8 = (f32[192,128]{0,1:T(8,128)S(1)}, f32[192,128]{0,1:T(8,128)S(1)}, u32[]{:S(2)}, u32[]{:S(2)}) collective-permute-start(f32[192,128]{0,1:T(8,128)S(1)} %get-tuple-element.21), channel_id=1, source_target_pairs={{0,1},{1,2},{2,3},{3,4},{4,5},{5,6},{6,7},{7,8},{8,9},{9,10},{10,1... | collective-permute-start | bytes 294920 | tf_op jit(solution)/shard_map/ppermute | solution.py:17
  56.9 7.1 %collective-permute-start.9 = (f32[192,128]{0,1:T(8,128)S(1)}, f32[192,128]{0,1:T(8,128)S(1)}, u32[]{:S(2)}, u32[]{:S(2)}) collective-permute-start(f32[192,128]{0,1:T(8,128)S(1)} %get-tuple-element.22), channel_id=1, source_target_pairs={{1,0},{2,1},{3,2},{4,3},{5,4},{6,5},{7,6},{8,7},{9,8},{10,9},{11,1... | collective-permute-start | bytes 294920 | tf_op jit(solution)/shard_map/ppermute | solution.py:19
where the time goes:
time: 67.7 us; the launch traced here: 67.3 us
  matrix products  20.3 us (30%)
  waiting for transfers between devices  19.5 us (29%)
  starting transfers between devices  11.4 us (17%)
  local copies, waits for them, and re-layouts  9.94 us (15%)
  other arithmetic  5.88 us (9%)
    ppermute x4, waiting for transfers between devices, extended_2(): lax.ppermute(head, axis, [((i + 1) % count, i) for i in range(count)])  12.5 us
    dot_general x2, matrix products, on_device(): jnp.einsum('bkij,bkjn->bin', transport, pieces, precision=lax.Precision.H...  11.3 us
    ppermute x4, starting transfers between devices, extended_2(): lax.ppermute(tail, axis, [(i, (i + 1) % count) for i in range(count)])  7.7 us
    gather x2, local copies, waits for them, and re-layouts, on_device(): fine_extended.reshape(-1, block_size, tracers)[columns]  7.25 us
    ppermute x2, waiting for transfers between devices, passed_along(): return lax.ppermute(block, axis, route)  5.13 us
    dot_general x2, matrix products, coarse_apply(): return jnp.dot(coarse_op, extended, precision=lax.Precision.HIGHEST)  3.71 us
    concatenate x2, other arithmetic, extended_2(): jnp.concatenate([lax.ppermute(tail, axis, [(i, (i + 1) % count) for i in...  3.29 us
    dot_general x2, matrix products, restrict(): lax.dot_general(onehot, values_in, (((0,), (0,)), ((), ())), precision=la...  3.22 us
  transfers between devices with their start and end apart: 10, of which 5 were waited for; matrix products, arithmetic and copies ran while one was open for 44% of the time, Pallas kernels for 0%

commit v1 on v0

v1 whole, which is shorter than its diff:
```python
import jax
import jax.numpy as jnp
from jax import lax
from jax.experimental import pallas as pl
from jax.experimental.pallas import tpu as pltpu
from jax.sharding import PartitionSpec as P

MESH = pl.DeviceIdType.MESH
HALO = 256
STEPS = 2
F32, BF16 = jnp.float32, jnp.bfloat16


def parts(x):
    high = x.astype(BF16)
    return high, (x - high.astype(F32)).astype(BF16)


def beside(x):
    return jnp.concatenate(parts(x), axis=1)


def dot(a, b):
    return jnp.dot(a, b, preferred_element_type=F32)


def kernel(
    starts, sources, ops, coarse_op, map_ref, cols, live, out,
    start_v, source_v, ops_v, coarse_v, ops_2, coarse_2, win, edge, halo,
    gather_m, spread_m, inverse, fine, fine_2, following, follow_src, jump, sent, state, image, result,
    load_sem, ops_sem, halo_send, halo_recv, tm_send, tm_recv, out_sem,
):
    tm, tile = lax.axis_index("tm"), lax.axis_index("tile")
    slices, tiles = lax.axis_size("tm"), lax.axis_size("tile")
    right, left = lax.rem(tile + 1, tiles), lax.rem(tile + tiles - 1, tiles)
    rows, tracers = starts.shape
    blocks, slots, size, _ = ops.shape
    coarse = coarse_op.shape[0]
    rim = state.shape[1]
    rim_blocks = HALO // size
    first, last = tm == 0, tm == slices - 1

    loads = [
        pltpu.make_async_copy(starts, start_v, load_sem.at[0]),
        pltpu.make_async_copy(sources, source_v, load_sem.at[1]),
        pltpu.make_async_copy(coarse_op, coarse_v, load_sem.at[2]),
    ]
    loads[0].start()

    def ops_load(b):
        return pltpu.make_async_copy(ops.at[b], ops_v.at[b], ops_sem.at[b])

    barrier = pltpu.get_barrier_semaphore()
    for other in (left, right):
        pl.semaphore_signal(barrier, inc=1, device_id=(tm, other), device_id_type=MESH)

    @pl.when(tm > 0)
    def _():
        pl.semaphore_signal(barrier, inc=1, device_id=(tm - 1, tile), device_id_type=MESH)

    @pl.when(tm < slices - 1)
    def _():
        pl.semaphore_signal(barrier, inc=1, device_id=(tm + 1, tile), device_id_type=MESH)

    @pl.loop(0, blocks)
    def _(b):
        ops_load(b).start()

    loads[1].start()
    loads[2].start()
    expected = 2 + jnp.where(first, 0, 1) + jnp.where(last, 0, 1)
    pl.semaphore_wait(barrier, expected)

    def halo_copies(step):
        if step == 0:
            head, tail = starts.at[pl.ds(0, HALO)], starts.at[pl.ds(rows - HALO, HALO)]
        else:
            head, tail = edge.at[step - 1, 0], edge.at[step - 1, 1]
        return [
            pltpu.make_async_remote_copy(
                src_ref=src, dst_ref=halo.at[step, side], send_sem=halo_send.at[step, side],
                recv_sem=halo_recv.at[step, side], device_id=(tm, to), device_id_type=MESH,
            )
            for side, src, to in ((0, tail, right), (1, head, left))
        ]

    exchanges = [halo_copies(step) for step in range(STEPS)]
    for copy in exchanges[0]:
        copy.start()

    hits = lax.broadcasted_iota(jnp.int32, (coarse, rows), 0) == map_ref[...]
    ones = jnp.where(hits, 1.0, 0.0)
    gather_m[...] = ones.astype(BF16)
    inverse[...] = jnp.broadcast_to(1.0 / jnp.sum(ones, axis=1, keepdims=True), (coarse, tracers))

    def restricted(low, high):
        both = dot(gather_m[low:high, :], fine_2[...])
        return (both[:, :tracers] + both[:, tracers:]) * inverse[low:high, :]

    loads[0].wait()

    @pl.loop(0, blocks)
    def _(b):
        here = pl.ds(pl.multiple_of(b * size, size), size)
        pair = beside(start_v[here, :])
        win[0, b + rim_blocks] = pair
        fine_2[here, :] = pair

    following_copy = pltpu.make_async_remote_copy(
        src_ref=follow_src, dst_ref=following, send_sem=tm_send.at[0], recv_sem=tm_recv.at[0],
        device_id=(lax.max(tm - 1, 0), tile), device_id_type=MESH,
    )
    follow_src[...] = restricted(0, coarse)

    @pl.when(tm > 0)
    def _():
        following_copy.start()

    @pl.loop(0, blocks)
    def _(b):
        ops_load(b).wait()
        for k in range(slots):
            kept = jnp.where(k < live[0, b], 1.0, 0.0)
            high, low = parts(ops_v[b, k] * kept)
            ops_2[b, 0:size, k * size:(k + 1) * size] = high
            ops_2[b, size:2 * size, k * size:(k + 1) * size] = low

    loads[1].wait()

    def take_halo(step):
        for side, copy in enumerate(exchanges[step]):
            copy.wait_recv()
            at = 0 if side == 0 else rim_blocks + blocks
            for i in range(rim_blocks):
                win[step, at + i] = beside(halo[step, side, i * size:(i + 1) * size, :])

    def row_block(step, b):
        pieces = jnp.concatenate([win[step, cols[k, b]] for k in range(slots)], axis=0)
        four = dot(ops_2[b], pieces)
        moved = four[:size, :tracers] + (four[:size, tracers:] + four[size:, :tracers])
        return moved + source_v[pl.ds(pl.multiple_of(b * size, size), size), :]

    def coarse_image():
        held = beside(state[...].reshape(4 * rim, tracers))
        four = dot(coarse_2[...], held)
        image[...] = four[:coarse, :tracers] + (four[:coarse, tracers:] + four[coarse:, :tracers])

    loads[2].wait()
    high, low = parts(coarse_v[...])
    coarse_2[0:coarse, :] = high
    coarse_2[coarse:, :] = low

    @pl.when(first)
    def _():
        state[...] = jnp.zeros(state.shape, F32)
        coarse_image()

    @pl.when(last)
    def _():
        following[...] = jnp.zeros(following.shape, F32)

    for step in range(STEPS - 1):
        take_halo(step)

        def edge_block(side, i):
            b = i if side == 0 else blocks - rim_blocks + i
            new = row_block(step, b)
            edge[step, side, i * size:(i + 1) * size, :] = new
            win[step + 1, b + rim_blocks] = beside(new)

        for side in (0, 1):
            for i in range(rim_blocks):
                edge_block(side, i)
            exchanges[step + 1][1 - side].start()

        @pl.loop(rim_blocks, blocks - rim_blocks)
        def _(b):
            win[step + 1, b + rim_blocks] = beside(row_block(step, b))

    @pl.loop(0, rows // size)
    def _(j):
        here = pl.ds(pl.multiple_of(j * size, size), size)
        lane = jnp.broadcast_to(map_ref[:, here].astype(F32), (size, size))
        column = jnp.transpose(lane).astype(jnp.int32)
        for g in range(coarse // size):
            want = lax.broadcasted_iota(jnp.int32, (size, size), 1) + g * size
            spread_m[here, g * size:(g + 1) * size] = jnp.where(column == want, 1.0, 0.0).astype(BF16)

    take_halo(STEPS - 1)

    @pl.loop(0, blocks)
    def _(b):
        new = row_block(STEPS - 1, b)
        here = pl.ds(pl.multiple_of(b * size, size), size)
        fine[here, :] = new
        fine_2[here, :] = beside(new)

    @pl.when(tm < slices - 1)
    def _():
        following_copy.wait_recv()

    following_tile = lax.min(tm + 1, slices - 1)
    state_copies = [
        pltpu.make_async_remote_copy(
            src_ref=sent.at[half], dst_ref=state.at[1 + half], send_sem=tm_send.at[1 + half],
            recv_sem=tm_recv.at[1 + half], device_id=(following_tile, tile), device_id_type=MESH,
        )
        for half in range(2)
    ]
    rim_copies = [
        pltpu.make_async_remote_copy(
            src_ref=state.at[1 + half], dst_ref=state.at[3 if half == 0 else 0], send_sem=tm_send.at[3 + half],
            recv_sem=tm_recv.at[3 + half], device_id=(tm, left if half == 0 else right), device_id_type=MESH,
        )
        for half in range(2)
    ]
    for half in (1, 0):
        span = slice(half * rim, (half + 1) * rim)
        jump[span, :] = restricted(half * rim, (half + 1) * rim) - following[span, :]

        @pl.when(first)
        def _():
            sent[half] = image[span, :] + jump[span, :]
            state_copies[half].start()

    @pl.when(tm > 0)
    def _():
        for half in (1, 0):
            state_copies[half].wait_recv()
            rim_copies[half].start()
        for half in (1, 0):
            rim_copies[half].wait_recv()
        coarse_image()

        @pl.when(tm < slices - 1)
        def _():
            for half in (1, 0):
                span = slice(half * rim, (half + 1) * rim)
                sent[half] = image[span, :] + jump[span, :]
                state_copies[half].start()

    pair = beside(image[...])
    pieces = out_sem.shape[0]
    some = rows // pieces
    stores = []
    for i in range(pieces):
        span = slice(i * some, (i + 1) * some)
        both = dot(spread_m[span, :], pair)
        result[span, :] = fine[span, :] + (both[:, :tracers] + both[:, tracers:])
        stores.append(pltpu.make_async_copy(result.at[pl.ds(i * some, some)], out.at[pl.ds(i * some, some)], out_sem.at[i]))
        stores[-1].start()

    for exchange in exchanges:
        for copy in exchange:
            copy.wait_send()

    @pl.when(tm > 0)
    def _():
        following_copy.wait_send()
        for copy in rim_copies:
            copy.wait_send()

    @pl.when(tm < slices - 1)
    def _():
        for copy in state_copies:
            copy.wait_send()

    for store in stores:
        store.wait()


def on_device(starts, sources, fine_ops, col_index, live_count, coarse_op, cell_map):
    rows, tracers = sources.shape
    _, blocks, slots, size, _ = fine_ops.shape
    coarse, wide = coarse_op.shape
    rim = (wide - coarse) // 2
    window = blocks + 2 * HALO // size
    anywhere = pl.BlockSpec(memory_space=pl.ANY)
    vmem = pl.BlockSpec(memory_space=pltpu.VMEM)
    smem = pl.BlockSpec(memory_space=pltpu.SMEM)
    dma = pltpu.SemaphoreType.DMA
    pieces = 4
    result = pl.pallas_call(
        kernel,
        out_shape=jax.ShapeDtypeStruct((rows, tracers), F32),
        in_specs=[anywhere, anywhere, anywhere, anywhere, vmem, smem, smem],
        out_specs=anywhere,
        scratch_shapes=[
            pltpu.VMEM((rows, tracers), F32),
            pltpu.VMEM((rows, tracers), F32),
            pltpu.VMEM((blocks, slots, size, size), F32),
            pltpu.VMEM((coarse, wide), F32),
            pltpu.VMEM((blocks, 2 * size, slots * size), BF16),
            pltpu.VMEM((2 * coarse, wide), BF16),
            pltpu.VMEM((STEPS, window, size, 2 * tracers), BF16),
            pltpu.VMEM((STEPS - 1, 2, HALO, tracers), F32),
            pltpu.VMEM((STEPS, 2, HALO, tracers), F32),
            pltpu.VMEM((coarse, rows), BF16),
            pltpu.VMEM((rows, coarse), BF16),
            pltpu.VMEM((coarse, tracers), F32),
            pltpu.VMEM((rows, tracers), F32),
            pltpu.VMEM((rows, 2 * tracers), BF16),
            pltpu.VMEM((coarse, tracers), F32),
            pltpu.VMEM((coarse, tracers), F32),
            pltpu.VMEM((coarse, tracers), F32),
            pltpu.VMEM((2, rim, tracers), F32),
            pltpu.VMEM((4, rim, tracers), F32),
            pltpu.VMEM((coarse, tracers), F32),
            pltpu.VMEM((rows, tracers), F32),
            dma((3,)),
            dma((blocks,)),
            dma((STEPS, 2)),
            dma((STEPS, 2)),
            dma((5,)),
            dma((5,)),
            dma((pieces,)),
        ],
        compiler_params=pltpu.CompilerParams(
            collective_id=0, has_side_effects=True, vmem_limit_bytes=48 * 2**20
        ),
    )(
        starts[0], sources, fine_ops[0], coarse_op, cell_map.reshape(1, rows), col_index[0].T, live_count,
    )
    return result[None]


def solution(mesh):
    placed = (
        P("tm", "tile", None),
        P("tile", None),
        P("tm", "tile", None, None, None),
        P("tm", "tile", None),
        P("tm", "tile"),
        P("tile", None),
        P("tile"),
    )
    return jax.shard_map(
        on_device, mesh=mesh, in_specs=placed, out_specs=P("tm", "tile", None), check_vma=False
    )
```

time: 67.7 us -> 35.9 us (0.53)
  Pallas kernels: 0 us -> 29.1 us
  matrix products: 20.3 us -> 0 us
  waiting for transfers between devices: 19.5 us -> 0 us
  starting transfers between devices: 11.4 us -> 0 us
  other arithmetic: 5.88 us -> 0 us
  local copies, waits for them, and re-layouts: 9.94 us -> 6.45 us
    pallas_call x0 -> x1, Pallas kernels: none -> 29.1 us  [on_device(): pl.pallas_call(kernel, out_shape=jax.ShapeDtypeStruct((rows, tracers), F3...]
    dot_general x7 -> x0, matrix products: 20.3 us -> none  [the longest x2 11.3 us: on_device(): jnp.einsum('bkij,bkjn->bin', transport, pieces, precision=lax.Precision.H...]
    ppermute x10 -> x0, waiting for transfers between devices: 19.5 us -> none  [the longest x4 12.5 us: extended_2(): lax.ppermute(head, axis, [((i + 1) % count, i) for i in range(count)])]
    ppermute x10 -> x0, starting transfers between devices: 11.4 us -> none  [the longest x4 7.7 us: extended_2(): lax.ppermute(tail, axis, [(i, (i + 1) % count) for i in range(count)])]
    gather x2 -> x0, local copies, waits for them, and re-layouts: 7.25 us -> none  [on_device(): fine_extended.reshape(-1, block_size, tracers)[columns]]
    unnamed x12 -> x11, local copies, waits for them, and re-layouts: 0.03 us -> 5.75 us
    concatenate x2 -> x0, other arithmetic: 3.29 us -> none  [extended_2(): jnp.concatenate([lax.ppermute(tail, axis, [(i, (i + 1) % count) for i in...]
    slice x4 -> x0, local copies, waits for them, and re-layouts: 2.4 us -> none  [extended_2(): lax.slice_in_dim(cells, cells.shape[dim] - width, cells.shape[dim], axis=...]
  transfers between devices with their start and end apart: 10 -> 0, of which waited for: 5 -> 0; matrix products, arithmetic and copies ran while one was open for 44% -> 0% of each run, Pallas kernels for 0% -> 0%
where the time goes in v1:
time: 35.9 us; the launch traced here: 35.6 us
  Pallas kernels  29.1 us (81%)
  local copies, waits for them, and re-layouts  6.45 us (18%)
    pallas_call x1, Pallas kernels, on_device(): pl.pallas_call(kernel, out_shape=jax.ShapeDtypeStruct((rows, tracers), F3...  29.1 us
    unnamed x11, local copies, waits for them, and re-layouts  5.75 us

profile of v1, /device:TPU:31, one launch (start us, length us, event | category | flops | bytes accessed | tf_op | source)
XLA Modules:
  0.0 35.6 jit_solution(12628229229453467147)
XLA Ops:
  0.0 0.7 %reshape.3.map_ref = s32[1,1536]{1,0:T(1,128)S(1)} reshape(s32[1536]{0:T(1024)} %param.13) | data formatting | bytes 12288 | tf_op jit(solution)/shard_map/reshape | solution.py:322
  0.7 0.0 copy-start
  0.7 1.3 %copy-done = f32[384,768]{1,0:T(8,128)S(1)} copy-done((f32[384,768]{1,0:T(8,128)S(1)}, f32[384,768]{1,0:T(8,128)}, u32[]{:S(2)}) %copy-start) | copy-done | bytes 1179672
  2.0 0.0 copy-start.1
  2.0 1.1 %copy-done.1 = f32[1,1536,128]{2,1,0:T(8,128)S(1)} copy-done((f32[1,1536,128]{2,1,0:T(8,128)S(1)}, f32[1,1536,128]{2,1,0:T(8,128)}, u32[]{:S(2)}) %copy-start.1) | copy-done | bytes 786456
  3.1 0.0 copy-start.2
  3.1 1.1 %copy-done.2 = f32[1536,128]{1,0:T(8,128)S(1)} copy-done((f32[1536,128]{1,0:T(8,128)S(1)}, f32[1536,128]{1,0:T(8,128)}, u32[]{:S(2)}) %copy-start.2) | copy-done | bytes 786456
  4.2 0.0 copy-start.3
  4.2 0.7 %copy-done.3 = s32[1,12,4]{1,2,0:T(4,128)S(1)} copy-done((s32[1,12,4]{1,2,0:T(4,128)S(1)}, s32[1,12,4]{1,2,0:T(4,128)}, u32[]{:S(2)}) %copy-start.3) | copy-done | bytes 216
  4.9 0.0 copy-start.4
  4.9 0.7 %copy-done.4 = s32[1,12]{1,0:T(1,128)S(1)} copy-done((s32[1,12]{1,0:T(1,128)S(1)}, s32[1,12]{1,0:T(1,128)}, u32[]{:S(2)}) %copy-start.4) | copy-done | bytes 72
  5.6 29.1 %shard_map.73 = f32[1536,128]{1,0:T(8,128)S(1)} custom-call(f32[1536,128]{1,0:T(8,128)S(1)} %bitcast.7, f32[1536,128]{1,0:T(8,128)S(1)} %copy-done.2, f32[12,4,128,128]{3,2,1,0:T(8,128)} %bitcast.9, f32[384,768]{1,0:T(8,128)S(1)} %copy-done, s32[1,1536]{1,0:T(1,128)S(1)} %reshape.3.map_ref, s32[4,12]{1,0:T(4,128)S(1)} %bitcast.8, s32[1,12]{1,0:T(1,128)S(1)} %copy-done.4), custom_call_target="tpu_custom_call" | custom-call | tf_op jit(solution)/shard_map/pallas_call | solution.py:283
  34.7 0.9 %copy.9 = f32[1,1536,128]{2,1,0:T(8,128)} copy(f32[1,1536,128]{2,1,0:T(8,128)S(1)} %bitcast.6) | data formatting | bytes 1572864
Async XLA Ops:
  0.7 1.3 %copy-start = (f32[384,768]{1,0:T(8,128)S(1)}, f32[384,768]{1,0:T(8,128)}, u32[]{:S(2)}) copy-start(f32[384,768]{1,0:T(8,128)} %coarse_op.1) | copy-start | bytes 3538948
  2.0 1.1 %copy-start.1 = (f32[1,1536,128]{2,1,0:T(8,128)S(1)}, f32[1,1536,128]{2,1,0:T(8,128)}, u32[]{:S(2)}) copy-start(f32[1,1536,128]{2,1,0:T(8,128)} %param.7) | copy-start | bytes 2359300
  3.1 1.1 %copy-start.2 = (f32[1536,128]{1,0:T(8,128)S(1)}, f32[1536,128]{1,0:T(8,128)}, u32[]{:S(2)}) copy-start(f32[1536,128]{1,0:T(8,128)} %sources.1) | copy-start | bytes 2359300
  4.2 0.7 %copy-start.3 = (s32[1,12,4]{1,2,0:T(4,128)S(1)}, s32[1,12,4]{1,2,0:T(4,128)}, u32[]{:S(2)}) copy-start(s32[1,12,4]{1,2,0:T(4,128)} %param.10) | copy-start | bytes 580
  4.9 0.7 %copy-start.4 = (s32[1,12]{1,0:T(1,128)S(1)}, s32[1,12]{1,0:T(1,128)}, u32[]{:S(2)}) copy-start(s32[1,12]{1,0:T(1,128)} %live.1) | copy-start | bytes 148

commit v2 on v1

--- a/solution.py
+++ b/solution.py
@@ -8,6 +8,7 @@
 MESH = pl.DeviceIdType.MESH
 HALO = 256
 STEPS = 2
+CHUNKS = 4
 F32, BF16 = jnp.float32, jnp.bfloat16
 
 
@@ -25,10 +26,10 @@
 
 
 def kernel(
-    starts, sources, ops, coarse_op, map_ref, cols, live, out,
-    start_v, source_v, ops_v, coarse_v, ops_2, coarse_2, win, edge, halo,
-    gather_m, spread_m, inverse, fine, fine_2, following, follow_src, jump, sent, state, image, result,
-    load_sem, ops_sem, halo_send, halo_recv, tm_send, tm_recv, out_sem,
+    starts, sources, ops, coarse_op, map_hbm, cols_hbm, live_hbm, out,
+    map_v, cols, live, start_v, source_v, ops_v, coarse_v, ops_2, coarse_own, coarse_rims, win, edge, halo,
+    gather_m, spread_m, inverse, fine, fine_2, following, follow_src, jump, sent, state, image,
+    load_sem, ops_sem, halo_send, halo_recv, tm_send, tm_recv,
 ):
     tm, tile = lax.axis_index("tm"), lax.axis_index("tile")
     slices, tiles = lax.axis_size("tm"), lax.axis_size("tile")
@@ -44,8 +45,12 @@
         pltpu.make_async_copy(starts, start_v, load_sem.at[0]),
         pltpu.make_async_copy(sources, source_v, load_sem.at[1]),
         pltpu.make_async_copy(coarse_op, coarse_v, load_sem.at[2]),
+        pltpu.make_async_copy(live_hbm, live, load_sem.at[3]),
+        pltpu.make_async_copy(cols_hbm, cols, load_sem.at[4]),
+        pltpu.make_async_copy(map_hbm, map_v, load_sem.at[5]),
     ]
-    loads[0].start()
+    for at in (0, 3, 4, 5):
+        loads[at].start()
 
     def ops_load(b):
         return pltpu.make_async_copy(ops.at[b], ops_v.at[b], ops_sem.at[b])
@@ -88,11 +93,6 @@
     for copy in exchanges[0]:
         copy.start()
 
-    hits = lax.broadcasted_iota(jnp.int32, (coarse, rows), 0) == map_ref[...]
-    ones = jnp.where(hits, 1.0, 0.0)
-    gather_m[...] = ones.astype(BF16)
-    inverse[...] = jnp.broadcast_to(1.0 / jnp.sum(ones, axis=1, keepdims=True), (coarse, tracers))
-
     def restricted(low, high):
         both = dot(gather_m[low:high, :], fine_2[...])
         return (both[:, :tracers] + both[:, tracers:]) * inverse[low:high, :]
@@ -106,15 +106,7 @@
         win[0, b + rim_blocks] = pair
         fine_2[here, :] = pair
 
-    following_copy = pltpu.make_async_remote_copy(
-        src_ref=follow_src, dst_ref=following, send_sem=tm_send.at[0], recv_sem=tm_recv.at[0],
-        device_id=(lax.max(tm - 1, 0), tile), device_id_type=MESH,
-    )
-    follow_src[...] = restricted(0, coarse)
-
-    @pl.when(tm > 0)
-    def _():
-        following_copy.start()
+    loads[3].wait()
 
     @pl.loop(0, blocks)
     def _(b):
@@ -126,6 +118,8 @@
             ops_2[b, size:2 * size, k * size:(k + 1) * size] = low
 
     loads[1].wait()
+    loads[4].wait()
+    loads[5].wait()
 
     def take_halo(step):
         for side, copy in enumerate(exchanges[step]):
@@ -140,24 +134,15 @@
         moved = four[:size, :tracers] + (four[:size, tracers:] + four[size:, :tracers])
         return moved + source_v[pl.ds(pl.multiple_of(b * size, size), size), :]
 
-    def coarse_image():
-        held = beside(state[...].reshape(4 * rim, tracers))
-        four = dot(coarse_2[...], held)
-        image[...] = four[:coarse, :tracers] + (four[:coarse, tracers:] + four[coarse:, :tracers])
-
-    loads[2].wait()
-    high, low = parts(coarse_v[...])
-    coarse_2[0:coarse, :] = high
-    coarse_2[coarse:, :] = low
-
-    @pl.when(first)
-    def _():
-        state[...] = jnp.zeros(state.shape, F32)
-        coarse_image()
-
-    @pl.when(last)
-    def _():
-        following[...] = jnp.zeros(following.shape, F32)
+    def coarse_part(operator, low, high):
+        held = beside(jnp.concatenate([state[low], state[high]], axis=0))
+        four = dot(operator[...], held)
+        return four[:coarse, :tracers] + (four[:coarse, tracers:] + four[coarse:, :tracers])
+
+    hits = lax.broadcasted_iota(jnp.int32, (coarse, rows), 0) == map_v[...].reshape(1, rows)
+    ones = jnp.where(hits, 1.0, 0.0)
+    gather_m[...] = ones.astype(BF16)
+    inverse[...] = jnp.broadcast_to(1.0 / jnp.sum(ones, axis=1, keepdims=True), (coarse, tracers))
 
     for step in range(STEPS - 1):
         take_halo(step)
@@ -177,10 +162,31 @@
         def _(b):
             win[step + 1, b + rim_blocks] = beside(row_block(step, b))
 
+    following_copy = pltpu.make_async_remote_copy(
+        src_ref=follow_src, dst_ref=following, send_sem=tm_send.at[0], recv_sem=tm_recv.at[0],
+        device_id=(lax.max(tm - 1, 0), tile), device_id_type=MESH,
+    )
+    follow_src[...] = restricted(0, coarse)
+
+    @pl.when(tm > 0)
+    def _():
+        following_copy.start()
+
+    loads[2].wait()
+    for at, part in enumerate(parts(coarse_v[...])):
+        here = slice(at * coarse, (at + 1) * coarse)
+        coarse_own[here, :] = part[:, rim:rim + coarse]
+        coarse_rims[here, :] = jnp.concatenate([part[:, :rim], part[:, rim + coarse:]], axis=1)
+
+    @pl.when(first)
+    def _():
+        state[...] = jnp.zeros(state.shape, F32)
+        image[...] = coarse_part(coarse_own, 1, 2) + coarse_part(coarse_rims, 0, 3)
+
     @pl.loop(0, rows // size)
     def _(j):
         here = pl.ds(pl.multiple_of(j * size, size), size)
-        lane = jnp.broadcast_to(map_ref[:, here].astype(F32), (size, size))
+        lane = jnp.broadcast_to(map_v[here].reshape(1, size).astype(F32), (size, size))
         column = jnp.transpose(lane).astype(jnp.int32)
         for g in range(coarse // size):
             want = lax.broadcasted_iota(jnp.int32, (size, size), 1) + g * size
@@ -200,55 +206,53 @@
         following_copy.wait_recv()
 
     following_tile = lax.min(tm + 1, slices - 1)
-    state_copies = [
-        pltpu.make_async_remote_copy(
-            src_ref=sent.at[half], dst_ref=state.at[1 + half], send_sem=tm_send.at[1 + half],
-            recv_sem=tm_recv.at[1 + half], device_id=(following_tile, tile), device_id_type=MESH,
+    share = rim // CHUNKS
+    order = [(half, chunk) for half in (1, 0) for chunk in range(CHUNKS)]
+    state_copies, rim_copies = {}, {}
+    for at, (half, chunk) in enumerate(order):
+        piece = pl.ds(chunk * share, share)
+        state_copies[half, chunk] = pltpu.make_async_remote_copy(
+            src_ref=sent.at[half, piece], dst_ref=state.at[1 + half, piece], send_sem=tm_send.at[1 + at],
+            recv_sem=tm_recv.at[1 + at], device_id=(following_tile, tile), device_id_type=MESH,
         )
-        for half in range(2)
-    ]
-    rim_copies = [
-        pltpu.make_async_remote_copy(
-            src_ref=state.at[1 + half], dst_ref=state.at[3 if half == 0 else 0], send_sem=tm_send.at[3 + half],
-            recv_sem=tm_recv.at[3 + half], device_id=(tm, left if half == 0 else right), device_id_type=MESH,
+        rim_copies[half, chunk] = pltpu.make_async_remote_copy(
+            src_ref=state.at[1 + half, piece], dst_ref=state.at[3 if half == 0 else 0, piece],
+            send_sem=tm_send.at[1 + 2 * CHUNKS + at], recv_sem=tm_recv.at[1 + 2 * CHUNKS + at],
+            device_id=(tm, left if half == 0 else right), device_id_type=MESH,
         )
-        for half in range(2)
-    ]
+
+    def send_state(half):
+        span = slice(half * rim, (half + 1) * rim)
+        sent[half] = image[span, :] + jump[span, :]
+        for chunk in range(CHUNKS):
+            state_copies[half, chunk].start()
+
     for half in (1, 0):
         span = slice(half * rim, (half + 1) * rim)
         jump[span, :] = restricted(half * rim, (half + 1) * rim) - following[span, :]
 
         @pl.when(first)
         def _():
-            sent[half] = image[span, :] + jump[span, :]
-            state_copies[half].start()
+            send_state(half)
 
     @pl.when(tm > 0)
     def _():
-        for half in (1, 0):
-            state_copies[half].wait_recv()
-            rim_copies[half].start()
-        for half in (1, 0):
-            rim_copies[half].wait_recv()
-        coarse_image()
+        for at in order:
+            state_copies[at].wait_recv()
+            rim_copies[at].start()
+        image[...] = coarse_part(coarse_own, 1, 2)
+        for at in order:
+            rim_copies[at].wait_recv()
+        image[...] += coarse_part(coarse_rims, 0, 3)
 
         @pl.when(tm < slices - 1)
         def _():
             for half in (1, 0):
-                span = slice(half * rim, (half + 1) * rim)
-                sent[half] = image[span, :] + jump[span, :]
-                state_copies[half].start()
+                send_state(half)
 
     pair = beside(image[...])
-    pieces = out_sem.shape[0]
-    some = rows // pieces
-    stores = []
-    for i in range(pieces):
-        span = slice(i * some, (i + 1) * some)
-        both = dot(spread_m[span, :], pair)
-        result[span, :] = fine[span, :] + (both[:, :tracers] + both[:, tracers:])
-        stores.append(pltpu.make_async_copy(result.at[pl.ds(i * some, some)], out.at[pl.ds(i * some, some)], out_sem.at[i]))
-        stores[-1].start()
+    both = dot(spread_m[...], pair)
+    out[...] = fine[...] + (both[:, :tracers] + both[:, tracers:])
 
     for exchange in exchanges:
         for copy in exchange:
@@ -257,16 +261,13 @@
     @pl.when(tm > 0)
     def _():
         following_copy.wait_send()
-        for copy in rim_copies:
+        for copy in rim_copies.values():
             copy.wait_send()
 
     @pl.when(tm < slices - 1)
     def _():
-        for copy in state_copies:
+        for copy in state_copies.values():
             copy.wait_send()
-
-    for store in stores:
-        store.wait()
 
 
 def on_device(starts, sources, fine_ops, col_index, live_count, coarse_op, cell_map):
@@ -275,23 +276,25 @@
     coarse, wide = coarse_op.shape
     rim = (wide - coarse) // 2
     window = blocks + 2 * HALO // size
-    anywhere = pl.BlockSpec(memory_space=pl.ANY)
+    anywhere = pl.BlockSpec(memory_space=pltpu.HBM)
     vmem = pl.BlockSpec(memory_space=pltpu.VMEM)
-    smem = pl.BlockSpec(memory_space=pltpu.SMEM)
     dma = pltpu.SemaphoreType.DMA
-    pieces = 4
     result = pl.pallas_call(
         kernel,
-        out_shape=jax.ShapeDtypeStruct((rows, tracers), F32),
-        in_specs=[anywhere, anywhere, anywhere, anywhere, vmem, smem, smem],
-        out_specs=anywhere,
+        out_shape=pltpu.VMEM((rows, tracers), F32),
+        in_specs=[anywhere] * 7,
+        out_specs=vmem,
         scratch_shapes=[
+            pltpu.VMEM((rows,), jnp.int32),
+            pltpu.SMEM((slots, blocks), jnp.int32),
+            pltpu.SMEM((1, blocks), jnp.int32),
             pltpu.VMEM((rows, tracers), F32),
             pltpu.VMEM((rows, tracers), F32),
             pltpu.VMEM((blocks, slots, size, size), F32),
             pltpu.VMEM((coarse, wide), F32),
             pltpu.VMEM((blocks, 2 * size, slots * size), BF16),
-            pltpu.VMEM((2 * coarse, wide), BF16),
+            pltpu.VMEM((2 * coarse, coarse), BF16),
+            pltpu.VMEM((2 * coarse, 2 * rim), BF16),
             pltpu.VMEM((STEPS, window, size, 2 * tracers), BF16),
             pltpu.VMEM((STEPS - 1, 2, HALO, tracers), F32),
             pltpu.VMEM((STEPS, 2, HALO, tracers), F32),
@@ -306,20 +309,18 @@
             pltpu.VMEM((2, rim, tracers), F32),
             pltpu.VMEM((4, rim, tracers), F32),
             pltpu.VMEM((coarse, tracers), F32),
-            pltpu.VMEM((rows, tracers), F32),
-            dma((3,)),
+            dma((6,)),
             dma((blocks,)),
             dma((STEPS, 2)),
             dma((STEPS, 2)),
-            dma((5,)),
-            dma((5,)),
-            dma((pieces,)),
+            dma((1 + 4 * CHUNKS,)),
+            dma((1 + 4 * CHUNKS,)),
         ],
         compiler_params=pltpu.CompilerParams(
-            collective_id=0, has_side_effects=True, vmem_limit_bytes=48 * 2**20
+            collective_id=0, has_side_effects=True, vmem_limit_bytes=56 * 2**20
         ),
     )(
-        starts[0], sources, fine_ops[0], coarse_op, cell_map.reshape(1, rows), col_index[0].T, live_count,
+        starts[0], sources, fine_ops[0], coarse_op, cell_map, col_index[0].T, live_count,
     )
     return result[None]
 

time: 35.9 us -> 28.5 us (0.79)
  the two profiles are of different devices: /device:TPU:31 before, /device:TPU:15 now
where the time goes in v2:
time: 28.5 us; the launch traced here: 28.4 us
  Pallas kernels  27.5 us (96%)
  local copies, waits for them, and re-layouts  0.88 us (3%)
    pallas_call x1, Pallas kernels, on_device(): pl.pallas_call(kernel, out_shape=pltpu.VMEM((rows, tracers), F32), in_spe...  27.5 us
    unnamed x1, local copies, waits for them, and re-layouts  0.88 us

profile of v2, /device:TPU:15, one launch (start us, length us, event | category | flops | bytes accessed | tf_op | source)
XLA Modules:
  0.0 28.4 jit_solution(7553301518899330590)
XLA Ops:
  0.0 27.5 %shard_map.73 = f32[1536,128]{1,0:T(8,128)S(1)} custom-call(f32[1536,128]{1,0:T(8,128)} %bitcast.8, f32[1536,128]{1,0:T(8,128)} %sources.1, f32[12,4,128,128]{3,2,1,0:T(8,128)} %bitcast.7, f32[384,768]{1,0:T(8,128)} %coarse_op.1, s32[1536]{0:T(1024)} %map_hbm.1, s32[4,12]{1,0:T(4,128)} %bitcast.9, s32[1,12]{1,0:T(1,128)} %live_hbm.1), custom_call_target="tpu_custom_call" | custom-call | tf_op jit(solution)/shard_map/pallas_call | solution.py:282
  27.5 0.9 %copy.9 = f32[1,1536,128]{2,1,0:T(8,128)} copy(f32[1,1536,128]{2,1,0:T(8,128)S(1)} %bitcast.6) | data formatting | bytes 1572864

commit v3 on v2

--- a/solution.py
+++ b/solution.py
@@ -144,24 +144,6 @@
     gather_m[...] = ones.astype(BF16)
     inverse[...] = jnp.broadcast_to(1.0 / jnp.sum(ones, axis=1, keepdims=True), (coarse, tracers))
 
-    for step in range(STEPS - 1):
-        take_halo(step)
-
-        def edge_block(side, i):
-            b = i if side == 0 else blocks - rim_blocks + i
-            new = row_block(step, b)
-            edge[step, side, i * size:(i + 1) * size, :] = new
-            win[step + 1, b + rim_blocks] = beside(new)
-
-        for side in (0, 1):
-            for i in range(rim_blocks):
-                edge_block(side, i)
-            exchanges[step + 1][1 - side].start()
-
-        @pl.loop(rim_blocks, blocks - rim_blocks)
-        def _(b):
-            win[step + 1, b + rim_blocks] = beside(row_block(step, b))
-
     following_copy = pltpu.make_async_remote_copy(
         src_ref=follow_src, dst_ref=following, send_sem=tm_send.at[0], recv_sem=tm_recv.at[0],
         device_id=(lax.max(tm - 1, 0), tile), device_id_type=MESH,
@@ -191,6 +173,24 @@
         for g in range(coarse // size):
             want = lax.broadcasted_iota(jnp.int32, (size, size), 1) + g * size
             spread_m[here, g * size:(g + 1) * size] = jnp.where(column == want, 1.0, 0.0).astype(BF16)
+
+    for step in range(STEPS - 1):
+        take_halo(step)
+
+        def edge_block(side, i):
+            b = i if side == 0 else blocks - rim_blocks + i
+            new = row_block(step, b)
+            edge[step, side, i * size:(i + 1) * size, :] = new
+            win[step + 1, b + rim_blocks] = beside(new)
+
+        for side in (0, 1):
+            for i in range(rim_blocks):
+                edge_block(side, i)
+            exchanges[step + 1][1 - side].start()
+
+        @pl.loop(rim_blocks, blocks - rim_blocks)
+        def _(b):
+            win[step + 1, b + rim_blocks] = beside(row_block(step, b))
 
     take_halo(STEPS - 1)
 

time: 28.5 us -> 27.4 us (0.961)
  the two profiles are of different devices: /device:TPU:15 before, /device:TPU:31 now
where the time goes in v3:
time: 27.4 us; the launch traced here: 27.2 us
  Pallas kernels  26.3 us (96%)
  local copies, waits for them, and re-layouts  0.88 us (3%)
    pallas_call x1, Pallas kernels, on_device(): pl.pallas_call(kernel, out_shape=pltpu.VMEM((rows, tracers), F32), in_spe...  26.3 us
    unnamed x1, local copies, waits for them, and re-layouts  0.88 us

profile of v3, /device:TPU:31, one launch (start us, length us, event | category | flops | bytes accessed | tf_op | source)
XLA Modules:
  0.0 27.2 jit_solution(3727147488276565930)
XLA Ops:
  0.0 26.3 %shard_map.73 = f32[1536,128]{1,0:T(8,128)S(1)} custom-call(f32[1536,128]{1,0:T(8,128)} %bitcast.8, f32[1536,128]{1,0:T(8,128)} %sources.1, f32[12,4,128,128]{3,2,1,0:T(8,128)} %bitcast.7, f32[384,768]{1,0:T(8,128)} %coarse_op.1, s32[1536]{0:T(1024)} %map_hbm.1, s32[4,12]{1,0:T(4,128)} %bitcast.9, s32[1,12]{1,0:T(1,128)} %live_hbm.1), custom_call_target="tpu_custom_call" | custom-call | tf_op jit(solution)/shard_map/pallas_call | solution.py:282
  26.3 0.9 %copy.9 = f32[1,1536,128]{2,1,0:T(8,128)} copy(f32[1,1536,128]{2,1,0:T(8,128)S(1)} %bitcast.6) | data formatting | bytes 1572864
